TPU v7x, 256 devices: a whole 4x4x8 slice. The times are simulated.
256 devices in a mesh: leaf: 64 (over y, x, z_lo), panel: 4 (over z_hi, core).
Axes of the slice: x: 4, y: 4, z: 8 (z_hi: 2, z_lo: 4; z = z_hi * 4 + z_lo), core: 2. Of those that a mesh axis runs over, the one named last changes fastest.
Arguments:
- child_front: bfloat16 [16384, 16384], P('leaf', 'panel'), may hold values from -6 to 6
- own_map: int32 [3, 64, 2], P(None, 'leaf'), may hold values from 0 to 1, each once within a row
- cross_map: int32 [3, 64, 2], P(None, 'leaf'), may hold values from 0 to 1, each once within a row
- pivot_inverse: bfloat16 [7, 512, 512], replicated, may hold values from -0.0029296875 to 0.0029296875
Outputs:
- schur: bfloat16 [16384, 16384], P('leaf', 'panel')
Inputs may be any that keep to these rules, and one draw needn't show every extreme that they name: Each own_map[k, d, :] is a permutation of the 2 blocks. Each cross_map[k, d, :] is a permutation of the 2 blocks.
All inputs are finite; a program needn't handle non-finite values.
Results may differ from a plain program's by a relative error of at most 0.0088.
Values may be sent and summed in bfloat16 or wider, within the bound.
A program may use at most 64 MiB of HBM per device.

v0:
```python
import jax
import jax.numpy as jnp
from jax import lax
from jax.sharding import PartitionSpec as P

PANEL = 512
BLOCK = 128


def swapped(block, axis, stride):
    count = lax.axis_size(axis)
    route = []
    for low in range(count):
        high = low | 1 << stride
        if high != low and high < count:
            route += [(low, high), (high, low)]
    return lax.ppermute(block, axis, route)


def spread(block, axis, owner):
    block = jnp.where(lax.axis_index(axis) == owner, block, jnp.zeros_like(block))
    return lax.psum(block, axis)


def extend_add(front_slab, partner, own_index, cross_index, block_count):
    slab_cols = front_slab.shape[1]
    slots = jnp.arange(block_count, dtype=jnp.int32)[None, :]
    own_table = (own_index[:, None] == slots).astype(jnp.bfloat16)
    cross_table = (cross_index[:, None] == slots).astype(jnp.bfloat16)
    own_blocks = front_slab.reshape(block_count, BLOCK, slab_cols)
    cross_blocks = partner.reshape(block_count, BLOCK, slab_cols)
    summed = jnp.einsum("sb,brc->src", own_table, own_blocks, preferred_element_type=jnp.float32)
    summed = summed + jnp.einsum(
        "sb,brc->src", cross_table, cross_blocks, preferred_element_type=jnp.float32
    )
    return summed.reshape(block_count * BLOCK, slab_cols).astype(jnp.bfloat16)


def collect_pivots(own_rows, leaf_index, group_bits):
    buffer = own_rows
    for step_bit in range(group_bits):
        received = swapped(buffer, "leaf", step_bit)
        upper_half = leaf_index >> step_bit & 1 == 1
        buffer = jnp.where(
            upper_half,
            jnp.concatenate([received, buffer], axis=0),
            jnp.concatenate([buffer, received], axis=0),
        )
    return buffer


def top_upper(own_rows, inverse, leaf_index, leaf_bits):
    pivots = collect_pivots(own_rows, leaf_index, leaf_bits)
    product = jnp.dot(inverse, pivots, preferred_element_type=jnp.float32)
    return product.astype(jnp.bfloat16)


def on_device(child_front, own_map, cross_map, pivot_inverse):
    leaf_count = lax.axis_size("leaf")
    leaf_bits = leaf_count.bit_length() - 1
    leaf_index = lax.axis_index("leaf")
    slab_rows = child_front.shape[0]
    block_count = slab_rows // BLOCK
    front_slab = child_front
    offsets = (0, 4, 6)
    for level_index in range(3):
        group_size = leaf_count // 2 ** (2 - level_index)
        group_bits = leaf_bits - 2 + level_index
        share_rows = PANEL // group_size
        partner = swapped(front_slab, "leaf", group_bits - 1)
        parent = extend_add(
            front_slab, partner, own_map[level_index, 0], cross_map[level_index, 0], block_count
        )
        front_number = offsets[level_index] + leaf_index // group_size
        inverse = lax.dynamic_index_in_dim(pivot_inverse, front_number, 0, keepdims=False)
        own_rows = parent[:share_rows]
        if level_index < 2:
            pivots = collect_pivots(own_rows, leaf_index, group_bits)
            upper_rows = jnp.dot(inverse, pivots, preferred_element_type=jnp.float32).astype(
                jnp.bfloat16
            )
        else:
            upper_rows = top_upper(own_rows, inverse, leaf_index, leaf_bits)
        columns = spread(parent[:, :PANEL], "panel", 0)
        reduced = parent.astype(jnp.float32) - jnp.dot(
            columns, upper_rows, preferred_element_type=jnp.float32
        )
        keep_mask = jnp.arange(slab_rows, dtype=jnp.int32)[:, None] >= share_rows
        front_slab = jnp.where(keep_mask, reduced, jnp.zeros_like(reduced)).astype(jnp.bfloat16)
    return front_slab


def solution(mesh):
    placed = (P("leaf", "panel"), P(None, "leaf", None), P(None, "leaf", None), P())
    return jax.shard_map(
        on_device, mesh=mesh, in_specs=placed, out_specs=P("leaf", "panel"), check_vma=False
    )
```

profile of v0, /device:TPU:1, one launch (start us, length us, event | category | flops | bytes accessed | tf_op | source)
XLA Modules:
  0.0 538.7 jit_solution(12298717727944464459)
XLA Ops:
  6.5 3.6 collective-permute-start
  10.1 1.0 slice_reduce_fusion.5
  11.1 1.0 slice_reduce_fusion
  12.1 4.0 fusion.34
  16.2 38.6 %collective-permute-done = bf16[256,4096]{1,0:T(8,128)(2,1)S(1)} collective-permute-done((bf16[256,4096]{1,0:T(8,128)(2,1)}, bf16[256,4096]{1,0:T(8,128)(2,1)S(1)}, u32[]{:S(2)}, u32[]{:S(2)}) %collective-permute-start) | collective-permute-done | bytes 2097184 | tf_op jit(solution)/shard_map/ppermute | solution.py:17
  54.7 3.0 fusion.6
  57.8 1.3 copy.14
  59.1 2.6 collective-permute-start.1
  61.7 5.1 collective-permute-done.1
  66.8 0.1 maximum_select_fusion.18
  66.9 3.0 collective-permute-start.2
  69.9 22.6 %collective-permute-done.2 = bf16[64,4096]{1,0:T(8,128)(2,1)} collective-permute-done((bf16[64,4096]{1,0:T(8,128)(2,1)S(1)}, bf16[64,4096]{1,0:T(8,128)(2,1)}, u32[]{:S(2)}, u32[]{:S(2)}) %collective-permute-start.2) | collective-permute-done | bytes 524320 | tf_op jit(solution)/shard_map/ppermute | solution.py:17
  92.5 1.9 maximum_select_fusion.15
  94.4 1.3 collective-permute-start.3
  95.7 22.0 %collective-permute-done.3 = bf16[128,4096]{1,0:T(8,128)(2,1)} collective-permute-done((bf16[128,4096]{1,0:T(8,128)(2,1)S(1)}, bf16[128,4096]{1,0:T(8,128)(2,1)}, u32[]{:S(2)}, u32[]{:S(2)}) %collective-permute-start.3) | collective-permute-done | bytes 1048608 | tf_op jit(solution)/shard_map/ppermute | solution.py:17
  117.7 3.4 maximum_select_fusion.12
  121.1 2.8 collective-permute-start.4
  123.9 0.7 slice_select_fusion.2
  124.6 0.0 all-reduce.4.cloned.1.call-update
  124.6 0.0 all-reduce.6.cloned.1.call-start
  124.7 57.9 %all-reduce.4.cloned.1.call-done = bf16[256,512]{1,0:T(8,128)(2,1)} async-done(((bf16[256,512]{1,0:T(8,128)(2,1)}), bf16[256,512]{1,0:T(8,128)(2,1)}) %all-reduce.4.cloned.1.call-update) | async-done | bytes 262160 | tf_op jit(solution)/shard_map/psum | solution.py:22
  182.6 7.2 %fusion.5 = bf16[256,4096]{1,0:T(8,128)(2,1)} fusion(bf16[256,512]{1,0:T(8,128)(2,1)} %all-reduce.4.cloned.1.call-done, bf16[256,4096]{1,0:T(8,128)(2,1)S(1)} %bitcast.44, bf16[256,4096]{1,0:T(8,128)(2,1)} %maximum_select_fusion.12, bf16[256,4096]{1,0:T(8,128)(2,1)} %collective-permute-done.4, pred[]{:T(512)S(6)} %eq.139, ...), kind=kOutput, calls=%fused_computation.14 | convolution fusion | flops 3246391296 | bytes 9175301 | tf_op jit(solution)/shard_map/dot_general | solution.py:85
  189.9 0.6 collective-permute-start.5
  190.5 4.1 fusion.31
  194.5 43.1 %collective-permute-done.5 = bf16[256,4096]{1,0:T(8,128)(2,1)S(1)} collective-permute-done((bf16[256,4096]{1,0:T(8,128)(2,1)}, bf16[256,4096]{1,0:T(8,128)(2,1)S(1)}, u32[]{:S(2)}, u32[]{:S(2)}) %collective-permute-start.5) | collective-permute-done | bytes 2097184 | tf_op jit(solution)/shard_map/ppermute | solution.py:17
  237.6 3.0 fusion.7
  240.6 1.3 copy.17
  241.9 0.1 collective-permute-start.6
  242.0 4.5 collective-permute-done.6
  246.6 0.1 collective-permute-start.7
  246.7 14.7 %collective-permute-done.7 = bf16[32,4096]{1,0:T(8,128)(2,1)S(1)} collective-permute-done((bf16[32,4096]{1,0:T(8,128)(2,1)S(1)}, bf16[32,4096]{1,0:T(8,128)(2,1)S(1)}, u32[]{:S(2)}, u32[]{:S(2)}) %collective-permute-start.7) | collective-permute-done | bytes 262176 | tf_op jit(solution)/shard_map/ppermute | solution.py:17
  261.4 0.1 maximum_select_fusion.19
  261.5 0.1 collective-permute-start.8
  261.6 13.0 %collective-permute-done.8 = bf16[64,4096]{1,0:T(8,128)(2,1)S(1)} collective-permute-done((bf16[64,4096]{1,0:T(8,128)(2,1)S(1)}, bf16[64,4096]{1,0:T(8,128)(2,1)S(1)}, u32[]{:S(2)}, u32[]{:S(2)}) %collective-permute-start.8) | collective-permute-done | bytes 524320 | tf_op jit(solution)/shard_map/ppermute | solution.py:17
  274.5 0.2 maximum_select_fusion.16
  274.8 1.1 collective-permute-start.9
  275.9 23.7 %collective-permute-done.9 = bf16[128,4096]{1,0:T(8,128)(2,1)S(1)} collective-permute-done((bf16[128,4096]{1,0:T(8,128)(2,1)S(1)}, bf16[128,4096]{1,0:T(8,128)(2,1)S(1)}, u32[]{:S(2)}, u32[]{:S(2)}) %collective-permute-start.9) | collective-permute-done | bytes 1048608 | tf_op jit(solution)/shard_map/ppermute | solution.py:17
  299.7 1.9 maximum_select_fusion.13
  301.6 0.7 slice_select_fusion.1
  302.4 0.0 all-reduce.6.cloned.1.call-update
  302.4 0.0 all-reduce.8.cloned.1.call-start
  302.5 52.4 %all-reduce.6.cloned.1.call-done = bf16[256,512]{1,0:T(8,128)(2,1)} async-done(((bf16[256,512]{1,0:T(8,128)(2,1)}), bf16[256,512]{1,0:T(8,128)(2,1)}) %all-reduce.6.cloned.1.call-update) | async-done | bytes 262160 | tf_op jit(solution)/shard_map/psum | solution.py:22
  354.9 7.2 %fusion.4 = bf16[256,4096]{1,0:T(8,128)(2,1)} fusion(bf16[256,512]{1,0:T(8,128)(2,1)} %all-reduce.6.cloned.1.call-done, bf16[256,4096]{1,0:T(8,128)(2,1)S(1)} %bitcast.47, bf16[256,4096]{1,0:T(8,128)(2,1)} %maximum_select_fusion.13, bf16[256,4096]{1,0:T(8,128)(2,1)} %collective-permute-done.10, pred[]{:T(512)S(6)} %eq.147, ...), kind=kOutput, calls=%fused_computation.13 | convolution fusion | flops 3246391296 | bytes 9175301 | tf_op jit(solution)/shard_map/dot_general | solution.py:85
  362.0 2.3 collective-permute-start.11
  364.3 4.1 fusion.28
  368.3 42.9 %collective-permute-done.11 = bf16[256,4096]{1,0:T(8,128)(2,1)S(1)} collective-permute-done((bf16[256,4096]{1,0:T(8,128)(2,1)}, bf16[256,4096]{1,0:T(8,128)(2,1)S(1)}, u32[]{:S(2)}, u32[]{:S(2)}) %collective-permute-start.11) | collective-permute-done | bytes 2097184 | tf_op jit(solution)/shard_map/ppermute | solution.py:17
  411.2 3.0 fusion.8
  414.2 1.3 copy.20
  415.6 0.1 collective-permute-start.12
  415.7 3.1 collective-permute-done.12
  418.8 0.1 collective-permute-start.13
  418.9 8.4 %collective-permute-done.13 = bf16[16,4096]{1,0:T(8,128)(2,1)S(1)} collective-permute-done((bf16[16,4096]{1,0:T(8,128)(2,1)S(1)}, bf16[16,4096]{1,0:T(8,128)(2,1)S(1)}, u32[]{:S(2)}, u32[]{:S(2)}) %collective-permute-start.13) | collective-permute-done | bytes 131104 | tf_op jit(solution)/shard_map/ppermute | solution.py:17
  427.4 0.1 collective-permute-start.14
  427.5 6.9 %collective-permute-done.14 = bf16[32,4096]{1,0:T(8,128)(2,1)S(1)} collective-permute-done((bf16[32,4096]{1,0:T(8,128)(2,1)S(1)}, bf16[32,4096]{1,0:T(8,128)(2,1)S(1)}, u32[]{:S(2)}, u32[]{:S(2)}) %collective-permute-start.14) | collective-permute-done | bytes 262176 | tf_op jit(solution)/shard_map/ppermute | solution.py:17
  434.3 0.1 maximum_select_fusion.20
  434.4 0.5 collective-permute-start.15
  434.9 12.7 %collective-permute-done.15 = bf16[64,4096]{1,0:T(8,128)(2,1)S(1)} collective-permute-done((bf16[64,4096]{1,0:T(8,128)(2,1)S(1)}, bf16[64,4096]{1,0:T(8,128)(2,1)S(1)}, u32[]{:S(2)}, u32[]{:S(2)}) %collective-permute-start.15) | collective-permute-done | bytes 524320 | tf_op jit(solution)/shard_map/ppermute | solution.py:17
  447.6 0.2 maximum_select_fusion.17
  447.9 0.1 collective-permute-start.16
  448.0 21.9 %collective-permute-done.16 = bf16[128,4096]{1,0:T(8,128)(2,1)S(1)} collective-permute-done((bf16[128,4096]{1,0:T(8,128)(2,1)S(1)}, bf16[128,4096]{1,0:T(8,128)(2,1)S(1)}, u32[]{:S(2)}, u32[]{:S(2)}) %collective-permute-start.16) | collective-permute-done | bytes 1048608 | tf_op jit(solution)/shard_map/ppermute | solution.py:17
  469.9 2.0 maximum_select_fusion.14
  471.8 0.7 slice_select_fusion
  472.6 52.5 %all-reduce.8.cloned.1.call-done = bf16[256,512]{1,0:T(8,128)(2,1)} async-done(((bf16[256,512]{1,0:T(8,128)(2,1)}), bf16[256,512]{1,0:T(8,128)(2,1)}) %all-reduce.8.cloned.1.call-update) | async-done | bytes 262160 | tf_op jit(solution)/shard_map/psum | solution.py:22
  525.1 7.1 %fusion.3 = bf16[256,4096]{1,0:T(8,128)(2,1)} fusion(bf16[256,512]{1,0:T(8,128)(2,1)} %all-reduce.8.cloned.1.call-done, bf16[256,4096]{1,0:T(8,128)(2,1)S(1)} %bitcast.50, bf16[256,4096]{1,0:T(8,128)(2,1)} %maximum_select_fusion.14, bf16[256,4096]{1,0:T(8,128)(2,1)} %collective-permute-done.17, pred[]{:T(512)S(6)} %eq.152, ...), kind=kOutput, calls=%fused_computation.12 | convolution fusion | flops 3246391296 | bytes 9175301 | tf_op jit(solution)/shard_map/dot_general | solution.py:85
  (18 shorter events, 0.2 us)
Async XLA Ops:
  6.5 176.1 %all-reduce.4.cloned.1.call-start = ((), (), s32[]{:S(2)}) async-start(), calls=%async_computation | async-start | bytes 524288 | tf_op jit(solution)/shard_map/psum | solution.py:22
  6.5 48.2 %collective-permute-start = (bf16[256,4096]{1,0:T(8,128)(2,1)}, bf16[256,4096]{1,0:T(8,128)(2,1)S(1)}, u32[]{:S(2)}, u32[]{:S(2)}) collective-permute-start(bf16[256,4096]{1,0:T(8,128)(2,1)} %param.4), channel_id=1, source_target_pairs={{0,32},{32,0},{4,36},{36,4},{8,40},{40,8},{12,44},{44,12},{16,48},... | collective-permute-start | bytes 6291464 | tf_op jit(solution)/shard_map/ppermute | solution.py:17
  59.1 7.7 %collective-permute-start.1 = (bf16[32,4096]{1,0:T(8,128)(2,1)S(1)}, bf16[32,4096]{1,0:T(8,128)(2,1)S(1)}, u32[]{:S(2)}, u32[]{:S(2)}) collective-permute-start(bf16[32,4096]{1,0:T(8,128)(2,1)S(1)} %slice.49), channel_id=1, source_target_pairs={{0,4},{4,0},{8,12},{12,8},{16,20},{20,16},{24,28},{28,24},{32,36},... | collective-permute-start | bytes 786440 | tf_op jit(solution)/shard_map/ppermute | solution.py:17
  66.9 3.0 copy-start
  66.9 25.6 %collective-permute-start.2 = (bf16[64,4096]{1,0:T(8,128)(2,1)S(1)}, bf16[64,4096]{1,0:T(8,128)(2,1)}, u32[]{:S(2)}, u32[]{:S(2)}) collective-permute-start(bf16[64,4096]{1,0:T(8,128)(2,1)S(1)} %maximum_select_fusion.18), channel_id=1, source_target_pairs={{0,8},{8,0},{4,12},{12,4},{16,24},{24,16},{20,28},{28,20},{32,40},... | collective-permute-start | bytes 1572872 | tf_op jit(solution)/shard_map/ppermute | solution.py:17
  94.4 23.3 %collective-permute-start.3 = (bf16[128,4096]{1,0:T(8,128)(2,1)S(1)}, bf16[128,4096]{1,0:T(8,128)(2,1)}, u32[]{:S(2)}, u32[]{:S(2)}) collective-permute-start(bf16[128,4096]{1,0:T(8,128)(2,1)S(1)} %maximum_select_fusion.15), channel_id=1, source_target_pairs={{0,16},{16,0},{4,20},{20,4},{8,24},{24,8},{12,28},{28,12},{32,48},... | collective-permute-start | bytes 3145736 | tf_op jit(solution)/shard_map/ppermute | solution.py:17
  121.1 61.5 %collective-permute-start.4 = (bf16[256,4096]{1,0:T(8,128)(2,1)}, bf16[256,4096]{1,0:T(8,128)(2,1)}, u32[]{:S(2)}, u32[]{:S(2)}) collective-permute-start(bf16[256,4096]{1,0:T(8,128)(2,1)} %maximum_select_fusion.12), channel_id=1, source_target_pairs={{0,32},{32,0},{4,36},{36,4},{8,40},{40,8},{12,44},{44,12},{16,48},... | collective-permute-start | bytes 6291464 | tf_op jit(solution)/shard_map/ppermute | solution.py:17
  124.6 230.2 %all-reduce.6.cloned.1.call-start = ((), (), s32[]{:S(2)}) async-start(), calls=%async_computation.1 | async-start | bytes 524288 | tf_op jit(solution)/shard_map/psum | solution.py:22
  189.9 47.7 %collective-permute-start.5 = (bf16[256,4096]{1,0:T(8,128)(2,1)}, bf16[256,4096]{1,0:T(8,128)(2,1)S(1)}, u32[]{:S(2)}, u32[]{:S(2)}) collective-permute-start(bf16[256,4096]{1,0:T(8,128)(2,1)} %fusion.5), channel_id=1, source_target_pairs={{0,64},{64,0},{4,68},{68,4},{8,72},{72,8},{12,76},{76,12},{16,80},... | collective-permute-start | bytes 6291464 | tf_op jit(solution)/shard_map/ppermute | solution.py:17
  241.9 4.6 collective-permute-start.6
  246.6 14.8 %collective-permute-start.7 = (bf16[32,4096]{1,0:T(8,128)(2,1)S(1)}, bf16[32,4096]{1,0:T(8,128)(2,1)S(1)}, u32[]{:S(2)}, u32[]{:S(2)}) collective-permute-start(bf16[32,4096]{1,0:T(8,128)(2,1)S(1)} %maximum_select_fusion.21), channel_id=1, source_target_pairs={{0,8},{8,0},{4,12},{12,4},{16,24},{24,16},{20,28},{28,20},{32,40},... | collective-permute-start | bytes 786440 | tf_op jit(solution)/shard_map/ppermute | solution.py:17
  261.5 13.1 %collective-permute-start.8 = (bf16[64,4096]{1,0:T(8,128)(2,1)S(1)}, bf16[64,4096]{1,0:T(8,128)(2,1)S(1)}, u32[]{:S(2)}, u32[]{:S(2)}) collective-permute-start(bf16[64,4096]{1,0:T(8,128)(2,1)S(1)} %maximum_select_fusion.19), channel_id=1, source_target_pairs={{0,16},{16,0},{4,20},{20,4},{8,24},{24,8},{12,28},{28,12},{32,48},... | collective-permute-start | bytes 1572872 | tf_op jit(solution)/shard_map/ppermute | solution.py:17
  274.8 24.9 %collective-permute-start.9 = (bf16[128,4096]{1,0:T(8,128)(2,1)S(1)}, bf16[128,4096]{1,0:T(8,128)(2,1)S(1)}, u32[]{:S(2)}, u32[]{:S(2)}) collective-permute-start(bf16[128,4096]{1,0:T(8,128)(2,1)S(1)} %maximum_select_fusion.16), channel_id=1, source_target_pairs={{0,32},{32,0},{4,36},{36,4},{8,40},{40,8},{12,44},{44,12},{16,48},... | collective-permute-start | bytes 3145736 | tf_op jit(solution)/shard_map/ppermute | solution.py:17
  301.6 53.2 %collective-permute-start.10 = (bf16[256,4096]{1,0:T(8,128)(2,1)}, bf16[256,4096]{1,0:T(8,128)(2,1)}, u32[]{:S(2)}, u32[]{:S(2)}) collective-permute-start(bf16[256,4096]{1,0:T(8,128)(2,1)} %maximum_select_fusion.13), channel_id=1, source_target_pairs={{0,64},{64,0},{4,68},{68,4},{8,72},{72,8},{12,76},{76,12},{16,80},... | collective-permute-start | bytes 6291464 | tf_op jit(solution)/shard_map/ppermute | solution.py:17
  302.4 222.7 %all-reduce.8.cloned.1.call-start = ((), (), s32[]{:S(2)}) async-start(), calls=%async_computation.2 | async-start | bytes 524288 | tf_op jit(solution)/shard_map/psum | solution.py:22
  362.0 49.2 %collective-permute-start.11 = (bf16[256,4096]{1,0:T(8,128)(2,1)}, bf16[256,4096]{1,0:T(8,128)(2,1)S(1)}, u32[]{:S(2)}, u32[]{:S(2)}) collective-permute-start(bf16[256,4096]{1,0:T(8,128)(2,1)} %fusion.4), channel_id=1, source_target_pairs={{0,128},{128,0},{4,132},{132,4},{8,136},{136,8},{12,140},{140,12},... | collective-permute-start | bytes 6291464 | tf_op jit(solution)/shard_map/ppermute | solution.py:17
  415.6 3.2 collective-permute-start.12
  418.8 8.5 %collective-permute-start.13 = (bf16[16,4096]{1,0:T(8,128)(2,1)S(1)}, bf16[16,4096]{1,0:T(8,128)(2,1)S(1)}, u32[]{:S(2)}, u32[]{:S(2)}) collective-permute-start(bf16[16,4096]{1,0:T(8,128)(2,1)S(1)} %maximum_select_fusion.23), channel_id=1, source_target_pairs={{0,8},{8,0},{4,12},{12,4},{16,24},{24,16},{20,28},{28,20},{32,40},... | collective-permute-start | bytes 393224 | tf_op jit(solution)/shard_map/ppermute | solution.py:17
  427.4 7.0 %collective-permute-start.14 = (bf16[32,4096]{1,0:T(8,128)(2,1)S(1)}, bf16[32,4096]{1,0:T(8,128)(2,1)S(1)}, u32[]{:S(2)}, u32[]{:S(2)}) collective-permute-start(bf16[32,4096]{1,0:T(8,128)(2,1)S(1)} %maximum_select_fusion.22), channel_id=1, source_target_pairs={{0,16},{16,0},{4,20},{20,4},{8,24},{24,8},{12,28},{28,12},{32,48},... | collective-permute-start | bytes 786440 | tf_op jit(solution)/shard_map/ppermute | solution.py:17
  434.4 13.2 %collective-permute-start.15 = (bf16[64,4096]{1,0:T(8,128)(2,1)S(1)}, bf16[64,4096]{1,0:T(8,128)(2,1)S(1)}, u32[]{:S(2)}, u32[]{:S(2)}) collective-permute-start(bf16[64,4096]{1,0:T(8,128)(2,1)S(1)} %maximum_select_fusion.20), channel_id=1, source_target_pairs={{0,32},{32,0},{4,36},{36,4},{8,40},{40,8},{12,44},{44,12},{16,48},... | collective-permute-start | bytes 1572872 | tf_op jit(solution)/shard_map/ppermute | solution.py:17
  447.9 22.0 %collective-permute-start.16 = (bf16[128,4096]{1,0:T(8,128)(2,1)S(1)}, bf16[128,4096]{1,0:T(8,128)(2,1)S(1)}, u32[]{:S(2)}, u32[]{:S(2)}) collective-permute-start(bf16[128,4096]{1,0:T(8,128)(2,1)S(1)} %maximum_select_fusion.17), channel_id=1, source_target_pairs={{0,64},{64,0},{4,68},{68,4},{8,72},{72,8},{12,76},{76,12},{16,80},... | collective-permute-start | bytes 3145736 | tf_op jit(solution)/shard_map/ppermute | solution.py:17
  471.8 53.2 %collective-permute-start.17 = (bf16[256,4096]{1,0:T(8,128)(2,1)}, bf16[256,4096]{1,0:T(8,128)(2,1)}, u32[]{:S(2)}, u32[]{:S(2)}) collective-permute-start(bf16[256,4096]{1,0:T(8,128)(2,1)} %maximum_select_fusion.14), channel_id=1, source_target_pairs={{0,128},{128,0},{4,132},{132,4},{8,136},{136,8},{12,140},{140,12},... | collective-permute-start | bytes 6291464 | tf_op jit(solution)/shard_map/ppermute | solution.py:17
Sparse Core Ops, SparseCore 0:
  124.8 57.8 all-reduce.3
  302.5 52.3 all-reduce.5
  472.7 52.3 all-reduce.7
where the time goes:
time: 539 us
  waiting for transfers between devices  446 us (83%)
  matrix products  42.6 us (8%)
  starting transfers between devices  18.4 us (3%)
  between operations  13.4 us (2%)
  other arithmetic  12.3 us (2%)
  local copies, waits for them, and re-layouts  6.04 us (1%)
    ppermute x18, waiting for transfers between devices, swapped(): return lax.ppermute(block, axis, route)  283 us
    psum x3, waiting for transfers between devices, spread(): return lax.psum(block, axis)  163 us
    dot_general x3, matrix products, on_device(): jnp.dot(columns, upper_rows, preferred_element_type=jnp.float32)  21.5 us
    ppermute x18, starting transfers between devices, swapped(): return lax.ppermute(block, axis, route)  18.3 us
    dot_general x3, matrix products, extend_add(): jnp.einsum('sb,brc->src', own_table, own_blocks, preferred_element_type=j...  12.1 us
  transfers between devices with their start and end apart: 21, of which 18 were waited for; matrix products, arithmetic and copies ran while one was open for 3% of the time, Pallas kernels for 0%

commit v1 on v0

--- a/solution.py
+++ b/solution.py
@@ -19,7 +19,8 @@
 
 def spread(block, axis, owner):
     block = jnp.where(lax.axis_index(axis) == owner, block, jnp.zeros_like(block))
-    return lax.psum(block, axis)
+    patches_make = lambda unit, mesh_dim: jnp.sum(lax.all_gather(unit, mesh_dim), axis=0)
+    return patches_make(block, axis)
 
 
 def extend_add(front_slab, partner, own_index, cross_index, block_count):

time: 539 us -> 493 us (0.915); the launches traced: 539 us -> 487 us
  waiting for transfers between devices: 446 us -> 371 us
  starting transfers between devices: 18.4 us -> 37.4 us
    psum x3 -> x0, waiting for transfers between devices: 163 us -> none  [spread(): return lax.psum(block, axis)]
    all_gather x0 -> x3, waiting for transfers between devices: none -> 111 us  [spread(): lax.all_gather(unit, mesh_dim)]
    ppermute x18, waiting for transfers between devices: 283 us -> 259 us  [swapped(): return lax.ppermute(block, axis, route)]
    ppermute x18, starting transfers between devices: 18.3 us -> 37.3 us  [swapped(): return lax.ppermute(block, axis, route)]
  transfers between devices with their start and end apart: 21 -> 21, of which waited for: 18 -> 20; matrix products, arithmetic and copies ran while one was open for 3% -> 4% of each run, Pallas kernels for 0% -> 0%
where the time goes in v1:
time: 493 us; the launch traced here: 487 us
  waiting for transfers between devices  371 us (75%)
  matrix products  42.4 us (9%)
  starting transfers between devices  37.4 us (8%)
  other arithmetic  16.7 us (3%)
  between operations  13.4 us (3%)
  local copies, waits for them, and re-layouts  6.04 us (1%)
    ppermute x18, waiting for transfers between devices, swapped(): return lax.ppermute(block, axis, route)  259 us
    all_gather x3, waiting for transfers between devices, spread(): lax.all_gather(unit, mesh_dim)  111 us
    ppermute x18, starting transfers between devices, swapped(): return lax.ppermute(block, axis, route)  37.3 us
    dot_general x3, matrix products, on_device(): jnp.dot(columns, upper_rows, preferred_element_type=jnp.float32)  21.2 us
    dot_general x3, matrix products, extend_add(): jnp.einsum('sb,brc->src', own_table, own_blocks, preferred_element_type=j...  12.1 us
    select_n x12, other arithmetic, collect_pivots(): jnp.where(upper_half, jnp.concatenate([received, buffer], axis=0), jnp.co...  10.2 us
  transfers between devices with their start and end apart: 21, of which 20 were waited for; matrix products, arithmetic and copies ran while one was open for 4% of the time, Pallas kernels for 0%

profile of v1, /device:TPU:1, one launch (start us, length us, event | category | flops | bytes accessed | tf_op | source)
XLA Modules:
  0.0 486.6 jit_solution(5400844020995580519)
XLA Ops:
  6.5 3.6 collective-permute-start
  10.1 1.0 slice_reduce_fusion.5
  11.1 1.0 slice_reduce_fusion
  12.1 4.0 fusion.34
  16.2 38.6 %collective-permute-done = bf16[256,4096]{1,0:T(8,128)(2,1)S(1)} collective-permute-done((bf16[256,4096]{1,0:T(8,128)(2,1)}, bf16[256,4096]{1,0:T(8,128)(2,1)S(1)}, u32[]{:S(2)}, u32[]{:S(2)}) %collective-permute-start) | collective-permute-done | bytes 2097184 | tf_op jit(solution)/shard_map/ppermute | solution.py:17
  54.7 3.0 fusion.6
  57.8 1.3 copy.14
  59.1 2.6 collective-permute-start.1
  61.7 5.1 %collective-permute-done.1 = bf16[32,4096]{1,0:T(8,128)(2,1)S(1)} collective-permute-done((bf16[32,4096]{1,0:T(8,128)(2,1)S(1)}, bf16[32,4096]{1,0:T(8,128)(2,1)S(1)}, u32[]{:S(2)}, u32[]{:S(2)}) %collective-permute-start.1) | collective-permute-done | bytes 262176 | tf_op jit(solution)/shard_map/ppermute | solution.py:17
  66.9 3.0 collective-permute-start.2
  69.9 22.6 %collective-permute-done.2 = bf16[64,4096]{1,0:T(8,128)(2,1)} collective-permute-done((bf16[64,4096]{1,0:T(8,128)(2,1)S(1)}, bf16[64,4096]{1,0:T(8,128)(2,1)}, u32[]{:S(2)}, u32[]{:S(2)}) %collective-permute-start.2) | collective-permute-done | bytes 524320 | tf_op jit(solution)/shard_map/ppermute | solution.py:17
  92.5 1.9 maximum_select_fusion.15
  94.4 1.3 collective-permute-start.3
  95.7 22.0 %collective-permute-done.3 = bf16[128,4096]{1,0:T(8,128)(2,1)} collective-permute-done((bf16[128,4096]{1,0:T(8,128)(2,1)S(1)}, bf16[128,4096]{1,0:T(8,128)(2,1)}, u32[]{:S(2)}, u32[]{:S(2)}) %collective-permute-start.3) | collective-permute-done | bytes 1048608 | tf_op jit(solution)/shard_map/ppermute | solution.py:17
  117.7 3.6 maximum_select_fusion.12
  121.2 2.8 collective-permute-start.4
  124.0 0.7 slice_select_fusion.2
  124.8 34.9 %all-gather.7.cloned.1.call-done = bf16[1024,512]{1,0:T(8,128)(2,1)} async-done(((bf16[256,512]{1,0:T(8,128)(2,1)}), bf16[1024,512]{1,0:T(8,128)(2,1)}) %all-gather.7.cloned.1.call-update) | async-done | bytes 1048592 | tf_op jit(solution)/shard_map/all_gather | solution.py:22
  159.7 1.5 reduce_sum.36
  161.2 6.5 %collective-permute-done.4 = bf16[256,4096]{1,0:T(8,128)(2,1)} collective-permute-done((bf16[256,4096]{1,0:T(8,128)(2,1)}, bf16[256,4096]{1,0:T(8,128)(2,1)}, u32[]{:S(2)}, u32[]{:S(2)}) %collective-permute-start.4) | collective-permute-done | bytes 2097184 | tf_op jit(solution)/shard_map/ppermute | solution.py:17
  167.7 7.1 %fusion.5 = bf16[256,4096]{1,0:T(8,128)(2,1)} fusion(bf16[256,512]{1,0:T(8,128)(2,1)S(1)} %reduce_sum.36, bf16[256,4096]{1,0:T(8,128)(2,1)S(1)} %bitcast.47, bf16[256,4096]{1,0:T(8,128)(2,1)} %maximum_select_fusion.12, bf16[256,4096]{1,0:T(8,128)(2,1)} %collective-permute-done.4, pred[]{:T(512)S(6)} %eq.139, pred[256]{0:T(512)(128)(4,1)S(1)} %iota_compare_fusion, ...), kind=kOutput, calls=%fused_computation.14 | convolution fusion | flops 3246391296 | bytes 9175301 | tf_op jit(solution)/shard_map/dot_general | solution.py:86
  174.8 1.2 collective-permute-start.5
  176.1 4.1 fusion.31
  180.1 38.6 %collective-permute-done.5 = bf16[256,4096]{1,0:T(8,128)(2,1)S(1)} collective-permute-done((bf16[256,4096]{1,0:T(8,128)(2,1)}, bf16[256,4096]{1,0:T(8,128)(2,1)S(1)}, u32[]{:S(2)}, u32[]{:S(2)}) %collective-permute-start.5) | collective-permute-done | bytes 2097184 | tf_op jit(solution)/shard_map/ppermute | solution.py:17
  218.8 3.0 fusion.7
  221.7 1.3 copy.17
  223.1 5.0 %collective-permute-start.6 = (bf16[16,4096]{1,0:T(8,128)(2,1)S(1)}, bf16[16,4096]{1,0:T(8,128)(2,1)S(1)}, u32[]{:S(2)}, u32[]{:S(2)}) collective-permute-start(bf16[16,4096]{1,0:T(8,128)(2,1)S(1)} %slice.51), channel_id=1, source_target_pairs={{0,4},{4,0},{8,12},{12,8},{16,20},{20,16},{24,28},{28,24},{32,36},... | collective-permute-start | bytes 393224 | tf_op jit(solution)/shard_map/ppermute | solution.py:17
  228.1 2.4 collective-permute-done.6
  230.5 3.3 collective-permute-start.7
  233.7 10.1 %collective-permute-done.7 = bf16[32,4096]{1,0:T(8,128)(2,1)S(1)} collective-permute-done((bf16[32,4096]{1,0:T(8,128)(2,1)S(1)}, bf16[32,4096]{1,0:T(8,128)(2,1)S(1)}, u32[]{:S(2)}, u32[]{:S(2)}) %collective-permute-start.7) | collective-permute-done | bytes 262176 | tf_op jit(solution)/shard_map/ppermute | solution.py:17
  244.0 1.3 collective-permute-start.8
  245.2 9.5 %collective-permute-done.8 = bf16[64,4096]{1,0:T(8,128)(2,1)S(1)} collective-permute-done((bf16[64,4096]{1,0:T(8,128)(2,1)S(1)}, bf16[64,4096]{1,0:T(8,128)(2,1)S(1)}, u32[]{:S(2)}, u32[]{:S(2)}) %collective-permute-start.8) | collective-permute-done | bytes 524320 | tf_op jit(solution)/shard_map/ppermute | solution.py:17
  254.7 0.2 maximum_select_fusion.16
  255.0 2.8 collective-permute-start.9
  257.8 21.6 %collective-permute-done.9 = bf16[128,4096]{1,0:T(8,128)(2,1)S(1)} collective-permute-done((bf16[128,4096]{1,0:T(8,128)(2,1)S(1)}, bf16[128,4096]{1,0:T(8,128)(2,1)S(1)}, u32[]{:S(2)}, u32[]{:S(2)}) %collective-permute-start.9) | collective-permute-done | bytes 1048608 | tf_op jit(solution)/shard_map/ppermute | solution.py:17
  279.4 1.9 maximum_select_fusion.13
  281.3 1.2 collective-permute-start.10
  282.5 0.7 slice_select_fusion.1
  283.3 33.6 %all-gather.9.cloned.1.call-done = bf16[1024,512]{1,0:T(8,128)(2,1)} async-done(((bf16[256,512]{1,0:T(8,128)(2,1)}), bf16[1024,512]{1,0:T(8,128)(2,1)}) %all-gather.9.cloned.1.call-update) | async-done | bytes 1048592 | tf_op jit(solution)/shard_map/all_gather | solution.py:22
  316.9 1.5 reduce_sum.37
  318.4 6.7 %collective-permute-done.10 = bf16[256,4096]{1,0:T(8,128)(2,1)} collective-permute-done((bf16[256,4096]{1,0:T(8,128)(2,1)}, bf16[256,4096]{1,0:T(8,128)(2,1)}, u32[]{:S(2)}, u32[]{:S(2)}) %collective-permute-start.10) | collective-permute-done | bytes 2097184 | tf_op jit(solution)/shard_map/ppermute | solution.py:17
  325.1 7.1 %fusion.4 = bf16[256,4096]{1,0:T(8,128)(2,1)} fusion(bf16[256,512]{1,0:T(8,128)(2,1)S(1)} %reduce_sum.37, bf16[256,4096]{1,0:T(8,128)(2,1)S(1)} %bitcast.50, bf16[256,4096]{1,0:T(8,128)(2,1)} %maximum_select_fusion.13, bf16[256,4096]{1,0:T(8,128)(2,1)} %collective-permute-done.10, pred[]{:T(512)S(6)} %eq.147, pred[256]{0:T(512)(128)(4,1)S(1)} %iota_compare_fusion.1, ...), kind=kOutput, calls=%fused_computation.13 | convolution fusion | flops 3246391296 | bytes 9175301 | tf_op jit(solution)/shard_map/dot_general | solution.py:86
  332.2 2.8 collective-permute-start.11
  335.0 4.1 fusion.28
  339.1 37.4 %collective-permute-done.11 = bf16[256,4096]{1,0:T(8,128)(2,1)S(1)} collective-permute-done((bf16[256,4096]{1,0:T(8,128)(2,1)}, bf16[256,4096]{1,0:T(8,128)(2,1)S(1)}, u32[]{:S(2)}, u32[]{:S(2)}) %collective-permute-start.11) | collective-permute-done | bytes 2097184 | tf_op jit(solution)/shard_map/ppermute | solution.py:17
  376.4 3.0 fusion.8
  379.4 1.3 copy.20
  380.8 0.4 collective-permute-start.12
  381.1 2.8 collective-permute-done.12
  384.0 2.2 collective-permute-start.13
  386.2 4.1 collective-permute-done.13
  390.3 0.1 collective-permute-start.14
  390.4 5.5 %collective-permute-done.14 = bf16[32,4096]{1,0:T(8,128)(2,1)S(1)} collective-permute-done((bf16[32,4096]{1,0:T(8,128)(2,1)S(1)}, bf16[32,4096]{1,0:T(8,128)(2,1)S(1)}, u32[]{:S(2)}, u32[]{:S(2)}) %collective-permute-start.14) | collective-permute-done | bytes 262176 | tf_op jit(solution)/shard_map/ppermute | solution.py:17
  396.0 0.1 collective-permute-start.15
  396.1 11.7 %collective-permute-done.15 = bf16[64,4096]{1,0:T(8,128)(2,1)S(1)} collective-permute-done((bf16[64,4096]{1,0:T(8,128)(2,1)S(1)}, bf16[64,4096]{1,0:T(8,128)(2,1)S(1)}, u32[]{:S(2)}, u32[]{:S(2)}) %collective-permute-start.15) | collective-permute-done | bytes 524320 | tf_op jit(solution)/shard_map/ppermute | solution.py:17
  407.8 0.2 maximum_select_fusion.17
  408.1 1.3 collective-permute-start.16
  409.3 14.2 %collective-permute-done.16 = bf16[128,4096]{1,0:T(8,128)(2,1)S(1)} collective-permute-done((bf16[128,4096]{1,0:T(8,128)(2,1)S(1)}, bf16[128,4096]{1,0:T(8,128)(2,1)S(1)}, u32[]{:S(2)}, u32[]{:S(2)}) %collective-permute-start.16) | collective-permute-done | bytes 1048608 | tf_op jit(solution)/shard_map/ppermute | solution.py:17
  423.5 2.0 maximum_select_fusion.14
  425.5 2.5 collective-permute-start.17
  428.0 0.7 slice_select_fusion
  428.8 42.8 %all-gather.11.cloned.1.call-done = bf16[1024,512]{1,0:T(8,128)(2,1)} async-done(((bf16[256,512]{1,0:T(8,128)(2,1)}), bf16[1024,512]{1,0:T(8,128)(2,1)}) %all-gather.11.cloned.1.call-update) | async-done | bytes 1048592 | tf_op jit(solution)/shard_map/all_gather | solution.py:22
  471.6 1.5 reduce_sum.38
  473.0 7.0 %fusion.3 = bf16[256,4096]{1,0:T(8,128)(2,1)} fusion(bf16[256,512]{1,0:T(8,128)(2,1)S(1)} %reduce_sum.38, bf16[256,4096]{1,0:T(8,128)(2,1)S(1)} %bitcast.53, bf16[256,4096]{1,0:T(8,128)(2,1)} %maximum_select_fusion.14, bf16[256,4096]{1,0:T(8,128)(2,1)} %collective-permute-done.17, pred[]{:T(512)S(6)} %eq.152, pred[256]{0:T(512)(128)(4,1)S(1)} %iota_compare_fusion.2, ...), kind=kOutput, calls=%fused_computation.12 | convolution fusion | flops 3246391296 | bytes 9175301 | tf_op jit(solution)/shard_map/dot_general | solution.py:86
  (21 shorter events, 0.6 us)
Async XLA Ops:
  6.5 153.2 %all-gather.7.cloned.1.call-start = ((), (), s32[]{:S(2)}) async-start(), calls=%async_computation | async-start | bytes 1310720 | tf_op jit(solution)/shard_map/all_gather | solution.py:22
  6.5 48.2 %collective-permute-start = (bf16[256,4096]{1,0:T(8,128)(2,1)}, bf16[256,4096]{1,0:T(8,128)(2,1)S(1)}, u32[]{:S(2)}, u32[]{:S(2)}) collective-permute-start(bf16[256,4096]{1,0:T(8,128)(2,1)} %param.4), channel_id=1, source_target_pairs={{0,32},{32,0},{4,36},{36,4},{8,40},{40,8},{12,44},{44,12},{16,48},... | collective-permute-start | bytes 6291464 | tf_op jit(solution)/shard_map/ppermute | solution.py:17
  59.1 7.7 %collective-permute-start.1 = (bf16[32,4096]{1,0:T(8,128)(2,1)S(1)}, bf16[32,4096]{1,0:T(8,128)(2,1)S(1)}, u32[]{:S(2)}, u32[]{:S(2)}) collective-permute-start(bf16[32,4096]{1,0:T(8,128)(2,1)S(1)} %slice.49), channel_id=1, source_target_pairs={{0,4},{4,0},{8,12},{12,8},{16,20},{20,16},{24,28},{28,24},{32,36},... | collective-permute-start | bytes 786440 | tf_op jit(solution)/shard_map/ppermute | solution.py:17
  66.9 3.0 copy-start
  66.9 25.6 %collective-permute-start.2 = (bf16[64,4096]{1,0:T(8,128)(2,1)S(1)}, bf16[64,4096]{1,0:T(8,128)(2,1)}, u32[]{:S(2)}, u32[]{:S(2)}) collective-permute-start(bf16[64,4096]{1,0:T(8,128)(2,1)S(1)} %maximum_select_fusion.18), channel_id=1, source_target_pairs={{0,8},{8,0},{4,12},{12,4},{16,24},{24,16},{20,28},{28,20},{32,40},... | collective-permute-start | bytes 1572872 | tf_op jit(solution)/shard_map/ppermute | solution.py:17
  94.4 23.3 %collective-permute-start.3 = (bf16[128,4096]{1,0:T(8,128)(2,1)S(1)}, bf16[128,4096]{1,0:T(8,128)(2,1)}, u32[]{:S(2)}, u32[]{:S(2)}) collective-permute-start(bf16[128,4096]{1,0:T(8,128)(2,1)S(1)} %maximum_select_fusion.15), channel_id=1, source_target_pairs={{0,16},{16,0},{4,20},{20,4},{8,24},{24,8},{12,28},{28,12},{32,48},... | collective-permute-start | bytes 3145736 | tf_op jit(solution)/shard_map/ppermute | solution.py:17
  121.2 46.5 %collective-permute-start.4 = (bf16[256,4096]{1,0:T(8,128)(2,1)}, bf16[256,4096]{1,0:T(8,128)(2,1)}, u32[]{:S(2)}, u32[]{:S(2)}) collective-permute-start(bf16[256,4096]{1,0:T(8,128)(2,1)} %maximum_select_fusion.12), channel_id=1, source_target_pairs={{0,32},{32,0},{4,36},{36,4},{8,40},{40,8},{12,44},{44,12},{16,48},... | collective-permute-start | bytes 6291464 | tf_op jit(solution)/shard_map/ppermute | solution.py:17
  124.7 192.2 %all-gather.9.cloned.1.call-start = ((), (), s32[]{:S(2)}) async-start(), calls=%async_computation.1 | async-start | bytes 1310720 | tf_op jit(solution)/shard_map/all_gather | solution.py:22
  174.8 43.9 %collective-permute-start.5 = (bf16[256,4096]{1,0:T(8,128)(2,1)}, bf16[256,4096]{1,0:T(8,128)(2,1)S(1)}, u32[]{:S(2)}, u32[]{:S(2)}) collective-permute-start(bf16[256,4096]{1,0:T(8,128)(2,1)} %fusion.5), channel_id=1, source_target_pairs={{0,64},{64,0},{4,68},{68,4},{8,72},{72,8},{12,76},{76,12},{16,80},... | collective-permute-start | bytes 6291464 | tf_op jit(solution)/shard_map/ppermute | solution.py:17
  223.1 7.3 %collective-permute-start.6 = (bf16[16,4096]{1,0:T(8,128)(2,1)S(1)}, bf16[16,4096]{1,0:T(8,128)(2,1)S(1)}, u32[]{:S(2)}, u32[]{:S(2)}) collective-permute-start(bf16[16,4096]{1,0:T(8,128)(2,1)S(1)} %slice.51), channel_id=1, source_target_pairs={{0,4},{4,0},{8,12},{12,8},{16,20},{20,16},{24,28},{28,24},{32,36},... | collective-permute-start | bytes 393224 | tf_op jit(solution)/shard_map/ppermute | solution.py:17
  230.5 13.4 %collective-permute-start.7 = (bf16[32,4096]{1,0:T(8,128)(2,1)S(1)}, bf16[32,4096]{1,0:T(8,128)(2,1)S(1)}, u32[]{:S(2)}, u32[]{:S(2)}) collective-permute-start(bf16[32,4096]{1,0:T(8,128)(2,1)S(1)} %maximum_select_fusion.21), channel_id=1, source_target_pairs={{0,8},{8,0},{4,12},{12,4},{16,24},{24,16},{20,28},{28,20},{32,40},... | collective-permute-start | bytes 786440 | tf_op jit(solution)/shard_map/ppermute | solution.py:17
  244.0 10.7 %collective-permute-start.8 = (bf16[64,4096]{1,0:T(8,128)(2,1)S(1)}, bf16[64,4096]{1,0:T(8,128)(2,1)S(1)}, u32[]{:S(2)}, u32[]{:S(2)}) collective-permute-start(bf16[64,4096]{1,0:T(8,128)(2,1)S(1)} %maximum_select_fusion.19), channel_id=1, source_target_pairs={{0,16},{16,0},{4,20},{20,4},{8,24},{24,8},{12,28},{28,12},{32,48},... | collective-permute-start | bytes 1572872 | tf_op jit(solution)/shard_map/ppermute | solution.py:17
  255.0 24.4 %collective-permute-start.9 = (bf16[128,4096]{1,0:T(8,128)(2,1)S(1)}, bf16[128,4096]{1,0:T(8,128)(2,1)S(1)}, u32[]{:S(2)}, u32[]{:S(2)}) collective-permute-start(bf16[128,4096]{1,0:T(8,128)(2,1)S(1)} %maximum_select_fusion.16), channel_id=1, source_target_pairs={{0,32},{32,0},{4,36},{36,4},{8,40},{40,8},{12,44},{44,12},{16,48},... | collective-permute-start | bytes 3145736 | tf_op jit(solution)/shard_map/ppermute | solution.py:17
  281.3 43.8 %collective-permute-start.10 = (bf16[256,4096]{1,0:T(8,128)(2,1)}, bf16[256,4096]{1,0:T(8,128)(2,1)}, u32[]{:S(2)}, u32[]{:S(2)}) collective-permute-start(bf16[256,4096]{1,0:T(8,128)(2,1)} %maximum_select_fusion.13), channel_id=1, source_target_pairs={{0,64},{64,0},{4,68},{68,4},{8,72},{72,8},{12,76},{76,12},{16,80},... | collective-permute-start | bytes 6291464 | tf_op jit(solution)/shard_map/ppermute | solution.py:17
  283.3 188.3 %all-gather.11.cloned.1.call-start = ((), (), s32[]{:S(2)}) async-start(), calls=%async_computation.2 | async-start | bytes 1310720 | tf_op jit(solution)/shard_map/all_gather | solution.py:22
  332.2 44.3 %collective-permute-start.11 = (bf16[256,4096]{1,0:T(8,128)(2,1)}, bf16[256,4096]{1,0:T(8,128)(2,1)S(1)}, u32[]{:S(2)}, u32[]{:S(2)}) collective-permute-start(bf16[256,4096]{1,0:T(8,128)(2,1)} %fusion.4), channel_id=1, source_target_pairs={{0,128},{128,0},{4,132},{132,4},{8,136},{136,8},{12,140},{140,12},... | collective-permute-start | bytes 6291464 | tf_op jit(solution)/shard_map/ppermute | solution.py:17
  380.8 3.2 collective-permute-start.12
  384.0 6.3 %collective-permute-start.13 = (bf16[16,4096]{1,0:T(8,128)(2,1)S(1)}, bf16[16,4096]{1,0:T(8,128)(2,1)S(1)}, u32[]{:S(2)}, u32[]{:S(2)}) collective-permute-start(bf16[16,4096]{1,0:T(8,128)(2,1)S(1)} %maximum_select_fusion.23), channel_id=1, source_target_pairs={{0,8},{8,0},{4,12},{12,4},{16,24},{24,16},{20,28},{28,20},{32,40},... | collective-permute-start | bytes 393224 | tf_op jit(solution)/shard_map/ppermute | solution.py:17
  390.3 5.6 %collective-permute-start.14 = (bf16[32,4096]{1,0:T(8,128)(2,1)S(1)}, bf16[32,4096]{1,0:T(8,128)(2,1)S(1)}, u32[]{:S(2)}, u32[]{:S(2)}) collective-permute-start(bf16[32,4096]{1,0:T(8,128)(2,1)S(1)} %maximum_select_fusion.22), channel_id=1, source_target_pairs={{0,16},{16,0},{4,20},{20,4},{8,24},{24,8},{12,28},{28,12},{32,48},... | collective-permute-start | bytes 786440 | tf_op jit(solution)/shard_map/ppermute | solution.py:17
  396.0 11.8 %collective-permute-start.15 = (bf16[64,4096]{1,0:T(8,128)(2,1)S(1)}, bf16[64,4096]{1,0:T(8,128)(2,1)S(1)}, u32[]{:S(2)}, u32[]{:S(2)}) collective-permute-start(bf16[64,4096]{1,0:T(8,128)(2,1)S(1)} %maximum_select_fusion.20), channel_id=1, source_target_pairs={{0,32},{32,0},{4,36},{36,4},{8,40},{40,8},{12,44},{44,12},{16,48},... | collective-permute-start | bytes 1572872 | tf_op jit(solution)/shard_map/ppermute | solution.py:17
  408.1 15.5 %collective-permute-start.16 = (bf16[128,4096]{1,0:T(8,128)(2,1)S(1)}, bf16[128,4096]{1,0:T(8,128)(2,1)S(1)}, u32[]{:S(2)}, u32[]{:S(2)}) collective-permute-start(bf16[128,4096]{1,0:T(8,128)(2,1)S(1)} %maximum_select_fusion.17), channel_id=1, source_target_pairs={{0,64},{64,0},{4,68},{68,4},{8,72},{72,8},{12,76},{76,12},{16,80},... | collective-permute-start | bytes 3145736 | tf_op jit(solution)/shard_map/ppermute | solution.py:17
  425.5 47.5 %collective-permute-start.17 = (bf16[256,4096]{1,0:T(8,128)(2,1)}, bf16[256,4096]{1,0:T(8,128)(2,1)}, u32[]{:S(2)}, u32[]{:S(2)}) collective-permute-start(bf16[256,4096]{1,0:T(8,128)(2,1)} %maximum_select_fusion.14), channel_id=1, source_target_pairs={{0,128},{128,0},{4,132},{132,4},{8,136},{136,8},{12,140},{140,12},... | collective-permute-start | bytes 6291464 | tf_op jit(solution)/shard_map/ppermute | solution.py:17
Sparse Core Ops, SparseCore 0:
  124.9 34.8 all-gather.6
  283.4 33.4 all-gather.8
  428.9 42.6 all-gather.10
